TPU v7x, 32 devices: a whole 2x2x4 slice. The times are simulated.
32 devices in a mesh: grp: 2 (over y), gx: 16 (over z, x, core).
Axes of the slice: x: 2, y: 2, z: 4, core: 2. Of those that a mesh axis runs over, the one named last changes fastest.
Arguments:
- features: bfloat16 [128, 32, 64, 128], P('grp', 'gx'), parts along dimension 0, may hold values from -6 to 6
- cotangent: bfloat16 [128, 32, 64, 128], P('grp', 'gx'), parts along dimension 0, may hold values from -6 to 6
- spectral_weight: bfloat16 [16384, 64, 128], P('gx'), may hold values from -0.5 to 0.5
- channel_weight: bfloat16 [64, 64], replicated, may hold values from -0.75 to 0.75
- channel_bias: float32 [64], replicated, may hold values from -3 to 3
Outputs:
- activated: bfloat16 [128, 32, 64, 128], P('grp', 'gx'), parts along dimension 0
- feature_grad: bfloat16 [128, 32, 64, 128], P('grp', 'gx'), parts along dimension 0
- spectral_grad: bfloat16 [32768, 64, 128], P(('grp', 'gx')), parts along dimension 0
There are 2 independent parts, one for each index of `grp`. A program takes and returns all parts, laid end to end along the dimension named above; an argument that names none is the same for every part. Nothing has to cross between parts.
All inputs are finite; a program needn't handle non-finite values.
Results may differ from a plain program's by a relative error of at most 0.018.
Values may be sent and summed in bfloat16 or wider, within the bound.
No kernel may reach another device: no remote copies, remote signals or barrier semaphores. Data moves between devices by JAX's collectives and lax.ppermute only.
A program may use at most 192 MiB of HBM per device.

v0:
```python
import functools
import math

import jax
import jax.numpy as jnp
import ml_dtypes
import numpy as np
from jax import lax
from jax.experimental import pallas as pl
from jax.experimental.pallas import tpu as pltpu
from jax.sharding import PartitionSpec as P

MX = 32
MY = 32
MZ = 16


SQRT_TWO_PI = math.sqrt(2.0 / math.pi)
CUBIC_COEF = 0.044715


def freq_index(retained, length):
    ladder = jnp.arange(retained, dtype=jnp.int32)
    return jnp.where(ladder < retained // 2, ladder, length - retained + ladder)


def cos_sin(wavenum, length):
    points = jnp.arange(length, dtype=jnp.int32)
    angles = (wavenum[:, None] * points[None, :] % length).astype(jnp.float32) * (
        2.0 * math.pi / length
    )
    return (jnp.cos(angles), jnp.sin(angles))


def analysis_pair(wavenum, length):
    cosine, sine_wave = cos_sin(wavenum, length)
    cosine, sine_wave = (cosine.T, sine_wave.T)
    return jnp.stack(
        [jnp.stack([cosine, -sine_wave], 1), jnp.stack([sine_wave, cosine], 1)], 1
    ).astype(jnp.bfloat16)


def synthesis_pair(wavenum, length):
    cosine, sine_wave = cos_sin(wavenum, length)
    return jnp.stack(
        [jnp.stack([cosine, sine_wave], 1), jnp.stack([-sine_wave, cosine], 1)], 1
    ).astype(jnp.bfloat16)


def depth_table(retained, length):
    cosine, sine_wave = cos_sin(jnp.arange(retained, dtype=jnp.int32), length)
    return jnp.concatenate([cosine, -sine_wave], 0).astype(jnp.bfloat16)


def gelu_parts(inputs):
    cubed_in = inputs * inputs * inputs
    tangent = jnp.tanh(SQRT_TWO_PI * (inputs + CUBIC_COEF * cubed_in))
    output = 0.5 * inputs * (1.0 + tangent)
    derivative = 0.5 * (1.0 + tangent) + 0.5 * inputs * (1.0 - tangent * tangent) * SQRT_TWO_PI * (
        1.0 + 3.0 * CUBIC_COEF * inputs * inputs
    )
    return (output, derivative)


def mode_product(coeffs, weights, channels):
    stacked = coeffs.reshape(coeffs.shape[0], 2, channels)
    halves = jnp.einsum("mac,mcj->amj", stacked, weights, preferred_element_type=jnp.float32)
    real_out = halves[0, :, :channels] - halves[1, :, channels:]
    imag_out = halves[0, :, channels:] + halves[1, :, :channels]
    return jnp.concatenate([real_out, imag_out], 1).astype(jnp.bfloat16)


def mode_grads(coeffs, weights, grad_modes, channels, weight_scale, input_scale):
    number = coeffs.shape[0]
    stacked = coeffs.reshape(number, 2, channels)
    grad_pairs = grad_modes.reshape(number, 2, channels)
    real_w = jnp.einsum("mac,mao->mco", stacked, grad_pairs, preferred_element_type=jnp.float32)
    imag_w = jnp.einsum(
        "mc,mo->mco", stacked[:, 0], grad_pairs[:, 1], preferred_element_type=jnp.float32
    ) - jnp.einsum(
        "mc,mo->mco", stacked[:, 1], grad_pairs[:, 0], preferred_element_type=jnp.float32
    )
    weight_grad = (jnp.concatenate([real_w, imag_w], 2) * weight_scale).astype(jnp.bfloat16)
    straight = jnp.concatenate([grad_pairs[:, 0], grad_pairs[:, 1]], 1)
    rotated = jnp.concatenate([grad_pairs[:, 1], -grad_pairs[:, 0]], 1)
    real_x = jnp.einsum("mcj,mj->mc", weights, straight, preferred_element_type=jnp.float32)
    imag_x = jnp.einsum("mcj,mj->mc", weights, rotated, preferred_element_type=jnp.float32)
    input_grad = (jnp.concatenate([real_x, imag_x], 1) * input_scale).astype(jnp.bfloat16)
    return (weight_grad, input_grad)


def general_body(features, cotangent, spectral_weight, channel_weight, channel_bias):
    channels, planes, lines, depth_len = features.shape
    devices = lax.axis_size("gx")
    all_planes = planes * devices
    owned_modes = spectral_weight.shape[0]
    wave_pairs = MY * MZ
    forward_scale = 1.0 / math.sqrt(all_planes * lines * depth_len)
    inverse_scale = 1.0 / math.sqrt(MX * wave_pairs)
    weight_scale = math.sqrt(MX * wave_pairs / (all_planes * lines * depth_len))
    depth_basis = depth_table(MZ, depth_len)
    across_y = analysis_pair(freq_index(MY, lines), lines)
    back_y = synthesis_pair(freq_index(MY, lines), lines)
    across_full = analysis_pair(freq_index(MX, all_planes), all_planes)
    back_full = synthesis_pair(freq_index(MX, all_planes), all_planes)
    depth_part = jnp.dot(features, depth_basis.T, preferred_element_type=jnp.float32).astype(
        jnp.bfloat16
    )
    plane_part = (
        jnp.einsum(
            "cxyaz,yabk->cxbkz",
            depth_part.reshape(channels, planes, lines, 2, MZ),
            across_y,
            preferred_element_type=jnp.float32,
        )
        .astype(jnp.bfloat16)
        .reshape(channels, planes, 2, wave_pairs)
    )
    all_rows = lax.all_to_all(plane_part, "gx", split_axis=3, concat_axis=1, tiled=True)
    mode_sums = jnp.einsum(
        "cxaq,xabk->qkbc", all_rows, across_full, preferred_element_type=jnp.float32
    ).reshape(owned_modes, 2 * channels)
    coeffs = (mode_sums * forward_scale).astype(jnp.bfloat16)
    spectral = mode_product(coeffs, spectral_weight, channels)
    planes_all = jnp.einsum(
        "qkao,kabx->oxbq",
        spectral.reshape(owned_modes // MX, MX, 2, channels),
        back_full,
        preferred_element_type=jnp.float32,
    ).astype(jnp.bfloat16)
    planes_back = lax.all_to_all(planes_all, "gx", split_axis=1, concat_axis=3, tiled=True)
    lines_back = (
        jnp.einsum(
            "oxakz,kaby->oxybz",
            planes_back.reshape(channels, planes, 2, MY, MZ),
            back_y,
            preferred_element_type=jnp.float32,
        )
        .astype(jnp.bfloat16)
        .reshape(channels, planes, lines, 2 * MZ)
    )
    spectral_term = (
        jnp.dot(lines_back, depth_basis, preferred_element_type=jnp.float32) * inverse_scale
    )
    pointwise = jnp.einsum(
        "oc,cxyz->oxyz", channel_weight, features, preferred_element_type=jnp.float32
    )
    hidden = spectral_term + pointwise + channel_bias[:, None, None, None]
    activated, derivative = gelu_parts(hidden)
    upstream = (cotangent.astype(jnp.float32) * derivative).astype(jnp.bfloat16)
    lines_grad = (
        jnp.dot(upstream, depth_basis.T, preferred_element_type=jnp.float32) * inverse_scale
    ).astype(jnp.bfloat16)
    rows_grad = (
        jnp.einsum(
            "oxybz,kaby->oxakz",
            lines_grad.reshape(channels, planes, lines, 2, MZ),
            back_y,
            preferred_element_type=jnp.float32,
        )
        .astype(jnp.bfloat16)
        .reshape(channels, planes, 2, wave_pairs)
    )
    all_grads = lax.all_to_all(rows_grad, "gx", split_axis=3, concat_axis=1, tiled=True)
    grad_sums = jnp.einsum(
        "oxbq,kabx->qkao", all_grads, back_full, preferred_element_type=jnp.float32
    ).reshape(owned_modes, 2 * channels)
    grad_modes = grad_sums.astype(jnp.bfloat16)
    spectral_grad, coeff_grad = mode_grads(
        coeffs, spectral_weight, grad_modes, channels, weight_scale, forward_scale
    )
    plane_all = jnp.einsum(
        "qkbc,xabk->cxaq",
        coeff_grad.reshape(owned_modes // MX, MX, 2, channels),
        across_full,
        preferred_element_type=jnp.float32,
    ).astype(jnp.bfloat16)
    plane_grad = lax.all_to_all(plane_all, "gx", split_axis=1, concat_axis=3, tiled=True)
    depth_grad = (
        jnp.einsum(
            "cxbkz,yabk->cxyaz",
            plane_grad.reshape(channels, planes, 2, MY, MZ),
            across_y,
            preferred_element_type=jnp.float32,
        )
        .astype(jnp.bfloat16)
        .reshape(channels, planes, lines, 2 * MZ)
    )
    channel_back = jnp.einsum(
        "oc,oxyz->cxyz", channel_weight, upstream, preferred_element_type=jnp.float32
    )
    feature_grad = (
        jnp.dot(depth_grad, depth_basis, preferred_element_type=jnp.float32) + channel_back
    ).astype(jnp.bfloat16)
    return (activated.astype(jnp.bfloat16), feature_grad, spectral_grad)


PLANES = 2
GROUP = 8
STEP = 16
VMEM_MIB = 40
NT = (((1,), (1,)), ((), ()))
F32 = jnp.float32
BF16 = jnp.bfloat16


def np_freq(retained, length):
    ladder = np.arange(retained)
    return np.where(ladder < retained // 2, ladder, length - retained + ladder)


def np_angles(wavenum, length):
    points = np.arange(length)
    return (wavenum[:, None] * points[None, :] % length) * (2.0 * math.pi / length)


def as_bf16(table):
    return np.asarray(table, np.float32).astype(ml_dtypes.bfloat16)


def rotation(angle, sign):
    cosine, sine_wave = np.cos(angle), sign * np.sin(angle)
    return np.stack([np.stack([cosine, -sine_wave]), np.stack([sine_wave, cosine])])


@functools.lru_cache(maxsize=None)
def tables(devices, lines, depth_len):
    planes_all = devices * PLANES
    angle = np_angles(np.arange(MZ), depth_len)
    depth = np.stack([np.cos(angle), -np.sin(angle)])
    eye = np.eye(GROUP)
    depth_block = np.einsum("akz,ij->akijz", depth, eye).reshape(2 * MZ * GROUP, GROUP * depth_len)
    plane_eye = np.eye(PLANES)
    angle = np_angles(np_freq(MY, lines), lines).reshape(devices, MY // devices, lines)
    across = np.einsum("badly,xw->ldbxawy", rotation(angle, -1.0), plane_eye)
    across = across.reshape(MY * 2 * PLANES, 2 * PLANES * lines)
    back = np.einsum("pbdly,xw->pxyldbw", rotation(angle, 1.0), plane_eye)
    back = back.reshape(2 * PLANES * lines, MY * 2 * PLANES)
    angle = np_angles(np_freq(MX, planes_all), planes_all).reshape(MX // 4, 4, devices, PLANES)
    forward = rotation(angle, -1.0)
    rows = np.einsum("batksx->tbksax", forward).reshape(MX // 4, 2, 4, devices * 2 * PLANES)
    plain = rows.reshape(2 * MX, -1)
    both = np.stack([rows, rows[:, ::-1]], 1).reshape(4 * MX, -1)
    turned = np.concatenate([rows[:, 1:], -rows[:, :1]], 1).reshape(2 * MX, -1)
    straight_rotated = np.concatenate([plain, turned], 0)
    inverse = np.einsum("batksx->sbxtak", rotation(angle, 1.0)).reshape(-1, 2 * MX)
    return {
        "depth": as_bf16(depth_block),
        "across_y": as_bf16(across),
        "back_y": as_bf16(back),
        "plain_x": as_bf16(plain),
        "both_x": as_bf16(both),
        "straight_x": as_bf16(straight_rotated),
        "back_x": as_bf16(inverse),
    }


def dot_nn(left, right):
    return jnp.dot(left, right, preferred_element_type=F32)


def dot_nt(left, right):
    return lax.dot_general(left, right, NT, preferred_element_type=F32)


def lanes(shape):
    return lax.broadcasted_iota(jnp.int32, shape, len(shape) - 1)


def sublanes(shape):
    return lax.broadcasted_iota(jnp.int32, shape, len(shape) - 2)


def swap_halves(block):
    return pltpu.roll(block, 64, 1)


def part_copy(source, target, sems, index, size):
    part = pl.ds(pl.multiple_of(index * size, size), size)
    return pltpu.make_async_copy(source.at[part], target.at[part], sems.at[index])


def start_parts(source, target, sems, size):
    for index in range(source.shape[0] // size):
        part_copy(source, target, sems, index, size).start()


def start_tables(pairs, sems):
    copies = []
    for index, (source, target) in enumerate(pairs):
        copy = pltpu.make_async_copy(source, target, sems.at[index])
        copy.start()
        copies.append(copy)
    return copies


def depth_analysis(slabs, depth, scale, group, lines_ref):
    wide = jnp.concatenate(slabs, axis=1)
    parts = dot_nt(depth, wide)
    if scale is not None:
        parts = parts * scale
    width = wide.shape[0]
    start = pl.multiple_of(group * GROUP, GROUP)
    for a in range(2):
        lines_ref[:, pl.ds(start, GROUP), a * width : (a + 1) * width] = parts[
            a * MZ * GROUP : (a + 1) * MZ * GROUP
        ].reshape(MZ, GROUP, width)


def rows_analysis(lines_ref, across_ref, rows_ref, out_ref):
    channels, width = lines_ref.shape[1], lines_ref.shape[2]
    across = across_ref[...]
    half = across.shape[0] // 2
    for kzh in range(MZ // 2):
        pair = lines_ref[2 * kzh : 2 * kzh + 2].reshape(2 * channels, width).astype(BF16)
        rows = dot_nt(across, pair)
        for kyl in range(2):
            rows_ref[pl.ds(kyl * 8 + kzh, half, stride=16), :] = rows[
                kyl * half : (kyl + 1) * half
            ]
    out_ref[...] = rows_ref[...].astype(BF16)


def rows_gather(block_ref, rows_ref, spec_ref):
    rows_ref[...] = block_ref[...].astype(F32)
    count = rows_ref.shape[0] // 16
    eye = (sublanes((128, 128)) == lanes((128, 128))).astype(BF16)
    for kzh in range(MZ // 2):
        both = jnp.concatenate(
            [rows_ref[pl.ds(kyl * 8 + kzh, count, stride=16), :] for kyl in range(2)], axis=0
        ).astype(BF16)
        turned = dot_nt(eye, both)
        for h in range(2):
            spec_ref[:, (2 * kzh + h) * GROUP : (2 * kzh + h + 1) * GROUP, :] = turned[
                h * 64 : (h + 1) * 64
            ].reshape(8, GROUP, turned.shape[1])


def synthesis(groups, spec_ref, back, depth, scale):
    wide = []
    for group in groups:
        lines = dot_nt(back, spec_ref[group].astype(BF16))
        if scale is not None:
            lines = lines * scale
        lines = lines.astype(BF16)
        half = lines.shape[0] // 2
        wide.append(jnp.concatenate([lines[:half], lines[half:]], axis=1))
    return dot_nn(jnp.concatenate(wide, axis=0), depth)


def flat(slab):
    return slab.reshape(slab.shape[0] * slab.shape[1], slab.shape[2])


def analysis_kernel(
    field_hbm,
    depth_hbm,
    across_hbm,
    out_ref,
    field_ref,
    depth_ref,
    across_ref,
    lines_ref,
    rows_ref,
    field_sems,
    table_sems,
):
    first, second = start_tables([(depth_hbm, depth_ref), (across_hbm, across_ref)], table_sems)
    start_parts(field_hbm, field_ref, field_sems, STEP)
    first.wait()

    @pl.loop(0, field_ref.shape[0] // STEP)
    def _(step):
        part_copy(field_hbm, field_ref, field_sems, step, STEP).wait()
        for g in range(STEP // GROUP):
            group = step * (STEP // GROUP) + g
            slabs = [flat(field_ref[group * GROUP + ci]) for ci in range(GROUP)]
            depth_analysis(slabs, depth_ref[...], None, group, lines_ref)

    second.wait()
    rows_analysis(lines_ref, across_ref, rows_ref, out_ref)


def middle_kernel(
    inverse_scale,
    block_ref,
    bias_ref,
    point_hbm,
    cot_hbm,
    depth_hbm,
    across_hbm,
    back_hbm,
    act_hbm,
    up_hbm,
    out_ref,
    point_ref,
    cot_ref,
    depth_ref,
    across_ref,
    back_ref,
    act_ref,
    up_ref,
    lines_ref,
    rows_ref,
    spec_ref,
    point_sems,
    cot_sems,
    act_sems,
    up_sems,
    table_sems,
):
    tables_in = start_tables(
        [(back_hbm, back_ref), (depth_hbm, depth_ref), (across_hbm, across_ref)], table_sems
    )
    start_parts(point_hbm, point_ref, point_sems, STEP)
    start_parts(cot_hbm, cot_ref, cot_sems, STEP)
    rows_gather(block_ref, rows_ref, spec_ref)
    for copy in tables_in:
        copy.wait()
    steps = point_ref.shape[0] // STEP

    @pl.loop(0, steps)
    def _(step):
        groups = [step * (STEP // GROUP) + g for g in range(STEP // GROUP)]
        spectral = synthesis(groups, spec_ref, back_ref[...], depth_ref[...], inverse_scale)
        part_copy(point_hbm, point_ref, point_sems, step, STEP).wait()
        part_copy(cot_hbm, cot_ref, cot_sems, step, STEP).wait()
        for g, group in enumerate(groups):
            slabs = []
            for oi in range(GROUP):
                index = group * GROUP + oi
                hidden = (
                    spectral[g * 128 : (g + 1) * 128, oi * 128 : (oi + 1) * 128]
                    + flat(point_ref[index]).astype(F32)
                    + bias_ref[index]
                )
                square = hidden * hidden
                gate = 0.5 + 0.5 * jnp.tanh(
                    hidden * (SQRT_TWO_PI + (SQRT_TWO_PI * CUBIC_COEF) * square)
                )
                slope = hidden * (2.0 * SQRT_TWO_PI + (6.0 * SQRT_TWO_PI * CUBIC_COEF) * square)
                derivative = gate + (gate - gate * gate) * slope
                upstream = (flat(cot_ref[index]).astype(F32) * derivative).astype(BF16)
                act_ref[index] = (hidden * gate).astype(BF16).reshape(act_ref.shape[1:])
                up_ref[index] = upstream.reshape(up_ref.shape[1:])
                slabs.append(upstream)
            depth_analysis(slabs, depth_ref[...], inverse_scale, group, lines_ref)
        part_copy(act_ref, act_hbm, act_sems, step, STEP).start()
        part_copy(up_ref, up_hbm, up_sems, step, STEP).start()

    rows_analysis(lines_ref, across_ref, rows_ref, out_ref)
    for step in range(steps):
        part_copy(act_ref, act_hbm, act_sems, step, STEP).wait()
        part_copy(up_ref, up_hbm, up_sems, step, STEP).wait()


def final_kernel(
    block_ref,
    point_hbm,
    depth_hbm,
    back_hbm,
    out_hbm,
    point_ref,
    depth_ref,
    back_ref,
    out_ref,
    rows_ref,
    spec_ref,
    point_sems,
    out_sems,
    table_sems,
):
    tables_in = start_tables([(back_hbm, back_ref), (depth_hbm, depth_ref)], table_sems)
    start_parts(point_hbm, point_ref, point_sems, STEP)
    rows_gather(block_ref, rows_ref, spec_ref)
    for copy in tables_in:
        copy.wait()
    steps = point_ref.shape[0] // STEP

    @pl.loop(0, steps)
    def _(step):
        groups = [step * (STEP // GROUP) + g for g in range(STEP // GROUP)]
        spectral = synthesis(groups, spec_ref, back_ref[...], depth_ref[...], None)
        part_copy(point_hbm, point_ref, point_sems, step, STEP).wait()
        for g, group in enumerate(groups):
            for ci in range(GROUP):
                index = group * GROUP + ci
                total = spectral[
                    g * 128 : (g + 1) * 128, ci * 128 : (ci + 1) * 128
                ] + flat(point_ref[index]).astype(F32)
                out_ref[index] = total.astype(BF16).reshape(out_ref.shape[1:])
        part_copy(out_ref, out_hbm, out_sems, step, STEP).start()

    for step in range(steps):
        part_copy(out_ref, out_hbm, out_sems, step, STEP).wait()


def point_kernel(
    transposed, weight_ref, field_hbm, out_hbm, field_ref, out_ref, wide_ref, in_sems, out_sems
):
    size = wide_ref.shape[0]
    planes = field_ref.shape[1]
    copies = []
    for plane in range(planes):
        part = (slice(None), pl.ds(plane, 1))
        copy = pltpu.make_async_copy(field_hbm.at[part], field_ref.at[part], in_sems.at[plane])
        copy.start()
        copies.append(copy)
    tall = (sublanes((size, 64)) // 16 == lanes((size, 64))).astype(BF16)
    weight = weight_ref[...]
    left = dot_nt(tall, weight) if transposed else dot_nn(tall, weight)
    left = left.astype(BF16)
    rows = size // 4
    same = sublanes((rows, size)) % 16 == lanes((rows, size)) % 16
    for quarter in range(4):
        spread = dot_nt(left[quarter * rows : (quarter + 1) * rows], tall)
        wide_ref[quarter * rows : (quarter + 1) * rows, :] = jnp.where(same, spread, 0.0).astype(
            BF16
        )
    sends = []
    for plane in range(planes):
        copies[plane].wait()
        for pair in range(2):
            right = jnp.concatenate(
                [
                    field_ref[:, plane, yc * 16 : (yc + 1) * 16, :].reshape(size, 128)
                    for yc in (2 * pair, 2 * pair + 1)
                ],
                axis=1,
            )
            result = dot_nn(wide_ref[...], right).astype(BF16)
            for k in range(2):
                yc = 2 * pair + k
                out_ref[:, plane, yc * 16 : (yc + 1) * 16, :] = result[
                    :, k * 128 : (k + 1) * 128
                ].reshape(size // 16, 16, 128)
        part = (slice(None), pl.ds(plane, 1))
        copy = pltpu.make_async_copy(out_ref.at[part], out_hbm.at[part], out_sems.at[plane])
        copy.start()
        sends.append(copy)
    for copy in sends:
        copy.wait()


def start_weights(weight_hbm, weight_ref, sems):
    copies = []
    for j in range(16):
        rows = weight_ref.shape[0] // 16
        part = pl.ds(j * rows, rows)
        copy = pltpu.make_async_copy(weight_hbm.at[part], weight_ref.at[part], sems.at[j])
        copy.start()
        copies.append(copy)
    return copies


def mode_pair(weight_ref, j, h, u):
    start = ((j * 2 + h) * MX + 8 * u) * 64
    return jnp.concatenate(
        [weight_ref[start : start + 256, :], weight_ref[start + 256 : start + 512, :]], axis=1
    )


def plane_sums(back_ref, mixed_ref, res_ref, out_ref):
    count = res_ref.shape[0] // 16
    for quarter in range(4):
        wide = jnp.concatenate([mixed_ref[quarter * 4 + k] for k in range(4)], axis=1)
        rows = dot_nn(back_ref[...], wide)
        for k in range(4):
            res_ref[pl.ds(quarter * 4 + k, count, stride=16), :] = rows[:, k * 128 : (k + 1) * 128]
    out_ref[...] = res_ref[...].astype(BF16)


def mode_kernel(
    scale,
    block_ref,
    weight_hbm,
    both_ref,
    plain_ref,
    back_ref,
    coeff_ref,
    out_ref,
    weight_ref,
    rows_ref,
    left_ref,
    mixed_ref,
    sems,
):
    copies = start_weights(weight_hbm, weight_ref, sems)
    count = rows_ref.shape[0] // 16
    rows_ref[...] = block_ref[...].astype(F32)
    low = lanes((128, 128)) < 64
    kxl = sublanes((128, 128)) % 4
    half = lanes((128, 128)) // 64
    first = (kxl == half).astype(BF16)
    second = (kxl == 2 + half).astype(BF16)
    low8 = lanes((8, 128)) < 64
    sign = jnp.where(sublanes((8, 128)) < 4, -1.0, 1.0)
    for quarter in range(4):
        wide = jnp.concatenate(
            [rows_ref[pl.ds(quarter * 4 + k, count, stride=16), :] for k in range(4)], axis=1
        ).astype(BF16)
        plain = (dot_nn(plain_ref[...], wide) * scale).astype(BF16)
        both = dot_nn(both_ref[...], wide) * scale
        for k in range(4):
            j = quarter * 4 + k
            coeff_ref[j] = plain[:, k * 128 : (k + 1) * 128]
            coeffs = both[:, k * 128 : (k + 1) * 128]
            swapped = swap_halves(coeffs)
            for h in range(2):
                twice = jnp.where(low if h == 0 else ~low, coeffs, swapped).astype(BF16)
                left_ref[j, h] = jnp.concatenate([twice * first, twice * second], axis=1)
    for j in range(16):
        if j % 4 == 0:
            for copy in copies[j : j + 4]:
                copy.wait()
        mixed = []
        for u in range(MX // 8):
            halves = [
                dot_nn(left_ref[j, h, u * 32 : (u + 1) * 32, :], mode_pair(weight_ref, j, h, u))
                for h in range(2)
            ]
            for t in range(2):
                low_h, high_h = [
                    part[t * 16 : (t + 1) * 16, t * 128 : (t + 1) * 128] for part in halves
                ]
                keep = jnp.where(low8, low_h[:8], sign * high_h[8:])
                move = jnp.where(low8, high_h[:8], sign * low_h[8:])
                mixed.append(keep + swap_halves(move))
        mixed_ref[j] = jnp.concatenate(mixed, axis=0).astype(BF16)
    plane_sums(back_ref, mixed_ref, rows_ref, out_ref)


def mode_grad_kernel(
    scale,
    block_ref,
    weight_hbm,
    straight_ref,
    back_ref,
    pair_ref,
    out_ref,
    weight_ref,
    rows_ref,
    mixed_ref,
    sems,
):
    copies = start_weights(weight_hbm, weight_ref, sems)
    count = rows_ref.shape[0] // 16
    rows_ref[...] = block_ref[...].astype(F32)
    low = lanes((64, 128)) < 64
    low16 = lanes((16, 128)) < 64
    row = sublanes((16, 128)) % 4
    upper = row < 2
    valid = lanes((16, 128)) // 64 == row % 2
    even = (sublanes((16, 128)) < 8).astype(BF16)
    odd = (sublanes((16, 128)) >= 8).astype(BF16)
    for j in range(16):
        section = rows_ref[pl.ds(j, count, stride=16), :]
        swapped = swap_halves(section)
        twice = jnp.concatenate(
            [jnp.where(low, section, swapped), jnp.where(low, swapped, section)], axis=1
        ).astype(BF16)
        turned = dot_nn(straight_ref[...], twice)
        for h in range(2):
            part = turned[:, h * 128 : (h + 1) * 128]
            pair_ref[2 * j + h] = jnp.where(low, part[:64], part[64:]).astype(BF16)
    for j in range(16):
        if j % 4 == 0:
            for copy in copies[j : j + 4]:
                copy.wait()
        mixed = []
        for u in range(MX // 8):
            found = []
            for h in range(2):
                pair = pair_ref[2 * j + h, u * 16 : (u + 1) * 16, :]
                rows = dot_nt(
                    jnp.concatenate([pair * even, pair * odd], axis=1),
                    mode_pair(weight_ref, j, h, u),
                )
                found.append(jnp.where(valid, jnp.where(upper, rows[:, :128], rows[:, 128:]), 0.0))
            keep = jnp.where(low16, found[0], found[1])
            move = jnp.where(low16, found[1], found[0])
            mixed.append(keep + swap_halves(move))
        mixed_ref[j] = (jnp.concatenate(mixed, axis=0) * scale).astype(BF16)
    plane_sums(back_ref, mixed_ref, rows_ref, out_ref)


def weight_grad_kernel(scale, coeff_ref, pair_ref, out_hbm, out_ref, mask_ref, sems):
    lane = lanes((128, 64))
    part = sublanes((128, 64)) // 64
    for t in range(MX // 4):
        mask_ref[t] = ((lane // 8 == t) & (lane % 4 // 2 == part)).astype(BF16)
    eye = (sublanes((128, 128)) == lanes((128, 128))).astype(BF16)
    even = (sublanes((64, 128)) % 2 == 0).astype(BF16)
    odd = (sublanes((64, 128)) % 2 == 1).astype(BF16)

    @pl.loop(0, 16)
    def _(j):
        turned = (dot_nt(eye, coeff_ref[j]) * scale).astype(BF16)
        for h in range(2):
            left = turned[h * 64 : (h + 1) * 64]
            left = jnp.concatenate([left, left], axis=0)
            pair = pair_ref[j * 2 + h]
            right = jnp.concatenate([pair * even, pair * odd], axis=1)
            for t in range(MX // 4):
                four = dot_nn(left * mask_ref[t], right).astype(BF16)
                mode = (j * 2 + h) * MX + 4 * t
                for k in range(4):
                    out_ref[mode + k] = four[
                        k // 2 * 64 : (k // 2 + 1) * 64, k % 2 * 128 : (k % 2 + 1) * 128
                    ]
        part_copy(out_ref, out_hbm, sems, j, 2 * MX).start()

    for j in range(16):
        part_copy(out_ref, out_hbm, sems, j, 2 * MX).wait()


def params(mib):
    return pltpu.CompilerParams(vmem_limit_bytes=mib * 1024 * 1024)


def cost(flops, moved):
    return pl.CostEstimate(flops=int(flops), bytes_accessed=int(moved), transcendentals=0)


def fast_body(features, cotangent, spectral_weight, channel_weight, channel_bias):
    channels, planes, lines, depth_len = features.shape
    devices = lax.axis_size("gx")
    owned_modes = spectral_weight.shape[0]
    wave_pairs = MY * MZ
    volume = planes * devices * lines * depth_len
    forward_scale = 1.0 / math.sqrt(volume)
    inverse_scale = 1.0 / math.sqrt(MX * wave_pairs)
    weight_scale = math.sqrt(MX * wave_pairs / volume)
    table = {name: jnp.asarray(value) for name, value in tables(devices, lines, depth_len).items()}
    block_rows = devices * 64
    block_shape = jax.ShapeDtypeStruct((block_rows, 128), BF16)
    vmem = pl.BlockSpec(memory_space=pltpu.VMEM)
    hbm = pl.BlockSpec(memory_space=pltpu.HBM)
    smem = pl.BlockSpec(memory_space=pltpu.SMEM)
    field_scratch = pltpu.VMEM(features.shape, BF16)
    field_shape = jax.ShapeDtypeStruct(features.shape, BF16)

    def sems(count):
        return pltpu.SemaphoreType.DMA((count,))

    def scratch(name):
        return pltpu.VMEM(table[name].shape, BF16)

    steps = channels // STEP
    lines_scratch = pltpu.VMEM((MZ, channels, 2 * planes * lines), F32)
    rows_scratch = pltpu.VMEM((block_rows, 128), F32)
    spec_scratch = pltpu.VMEM((channels // GROUP, MZ * GROUP, 128), F32)
    weight_rows = spectral_weight.reshape(owned_modes * channels, 2 * channels)
    field_bytes = features.size * 2

    def exchange(block):
        return lax.all_to_all(
            block.reshape(devices, 64, 128), "gx", 0, 0, tiled=True
        ).reshape(block_rows, 128)

    def point(field, transposed):
        return pl.pallas_call(
            functools.partial(point_kernel, transposed),
            out_shape=field_shape,
            in_specs=[vmem, hbm],
            out_specs=hbm,
            scratch_shapes=[
                field_scratch,
                field_scratch,
                pltpu.VMEM((channels * 16, channels * 16), BF16),
                sems(planes),
                sems(planes),
            ],
            compiler_params=params(VMEM_MIB),
            cost_estimate=cost(2 * 1024**3, 2 * field_bytes),
            name="channel_map_back" if transposed else "channel_map",
        )(channel_weight, field)

    block = pl.pallas_call(
        analysis_kernel,
        out_shape=block_shape,
        in_specs=[hbm, hbm, hbm],
        out_specs=vmem,
        scratch_shapes=[
            field_scratch,
            scratch("depth"),
            scratch("across_y"),
            lines_scratch,
            rows_scratch,
            sems(steps),
            sems(2),
        ],
        compiler_params=params(62),
        cost_estimate=cost(2 * 256 * 1024 * 1024, field_bytes),
        name="field_analysis",
    )(features, table["depth"], table["across_y"])
    block, pointwise = lax.optimization_barrier((exchange(block), point(features, False)))

    weight_scratch = pltpu.VMEM(weight_rows.shape, BF16)
    mixed_scratch = pltpu.VMEM((16, 64, 128), BF16)
    weight_sems = sems(16)
    coeffs, block = pl.pallas_call(
        functools.partial(mode_kernel, forward_scale),
        out_shape=[jax.ShapeDtypeStruct((16, 64, 128), BF16), block_shape],
        in_specs=[vmem, hbm, vmem, vmem, vmem],
        out_specs=[vmem, vmem],
        scratch_shapes=[
            weight_scratch,
            rows_scratch,
            pltpu.VMEM((16, 2, 128, 256), BF16),
            mixed_scratch,
            weight_sems,
        ],
        compiler_params=params(VMEM_MIB),
        cost_estimate=cost(256 * 2 * 16 * 256 * 128, 17 * 2**20),
        name="mode_product",
    )(block, weight_rows, table["both_x"], table["plain_x"], table["back_x"])
    block = exchange(block)

    activated, upstream, block = pl.pallas_call(
        functools.partial(middle_kernel, inverse_scale),
        out_shape=[field_shape, field_shape, block_shape],
        in_specs=[vmem, smem, hbm, hbm, hbm, hbm, hbm],
        out_specs=[hbm, hbm, vmem],
        scratch_shapes=[
            field_scratch,
            field_scratch,
            scratch("depth"),
            scratch("across_y"),
            scratch("back_y"),
            field_scratch,
            field_scratch,
            lines_scratch,
            rows_scratch,
            spec_scratch,
            sems(steps),
            sems(steps),
            sems(steps),
            sems(steps),
            sems(3),
        ],
        compiler_params=params(VMEM_MIB),
        cost_estimate=cost(2**30, 4 * field_bytes),
        name="gelu_and_gradient",
    )(
        block,
        channel_bias,
        pointwise,
        cotangent,
        table["depth"],
        table["across_y"],
        table["back_y"],
    )
    block = exchange(block)
    block, channel_back = lax.optimization_barrier((block, point(upstream, True)))

    pairs, block = pl.pallas_call(
        functools.partial(mode_grad_kernel, forward_scale),
        out_shape=[jax.ShapeDtypeStruct((32, 64, 128), BF16), block_shape],
        in_specs=[vmem, hbm, vmem, vmem],
        out_specs=[vmem, vmem],
        scratch_shapes=[weight_scratch, rows_scratch, mixed_scratch, weight_sems],
        compiler_params=params(VMEM_MIB),
        cost_estimate=cost(256 * 2 * 16 * 256 * 128, 17 * 2**20),
        name="mode_gradient",
    )(block, weight_rows, table["straight_x"], table["back_x"])
    block = exchange(block)

    spectral_grad = pl.pallas_call(
        functools.partial(weight_grad_kernel, weight_scale),
        out_shape=jax.ShapeDtypeStruct(spectral_weight.shape, BF16),
        in_specs=[vmem, vmem],
        out_specs=hbm,
        scratch_shapes=[
            pltpu.VMEM(spectral_weight.shape, BF16),
            pltpu.VMEM((MX // 4, 128, 64), BF16),
            sems(16),
        ],
        compiler_params=params(VMEM_MIB),
        cost_estimate=cost(512 * 2 * 64 * 64 * 256, 17 * 2**20),
        name="weight_gradient",
    )(coeffs, pairs)

    feature_grad = pl.pallas_call(
        final_kernel,
        out_shape=field_shape,
        in_specs=[vmem, hbm, hbm, hbm],
        out_specs=hbm,
        scratch_shapes=[
            field_scratch,
            scratch("depth"),
            scratch("back_y"),
            field_scratch,
            rows_scratch,
            spec_scratch,
            sems(steps),
            sems(steps),
            sems(2),
        ],
        compiler_params=params(VMEM_MIB),
        cost_estimate=cost(2**29, 2 * field_bytes),
        name="field_gradient",
    )(block, channel_back, table["depth"], table["back_y"])
    return (activated, feature_grad, spectral_grad)


def body(features, cotangent, spectral_weight, channel_weight, channel_bias):
    channels, planes, lines, depth_len = features.shape
    devices = lax.axis_size("gx")
    fits = (
        (channels, planes, lines, depth_len) == (64, PLANES, 64, 128)
        and spectral_weight.shape[0] == 2 * MZ * MX
        and devices * 2 == MY
        and devices * 2 == MX
    )
    run = fast_body if fits else general_body
    return run(features, cotangent, spectral_weight, channel_weight, channel_bias)


def solution(mesh):
    in_specs = (
        P("grp", "gx", None, None),
        P("grp", "gx", None, None),
        P("gx", None, None),
        P(),
        P(),
    )
    out_specs = (
        P("grp", "gx", None, None),
        P("grp", "gx", None, None),
        P(("grp", "gx"), None, None),
    )
    return jax.shard_map(body, mesh=mesh, in_specs=in_specs, out_specs=out_specs, check_vma=False)
```

profile of v0, /device:TPU:0, one launch (start us, length us, event | category | flops | bytes accessed | tf_op | source)
XLA Modules:
  0.0 94.6 jit_solution(5170386815630010312)
XLA Ops:
  0.6 4.3 %field_analysis.1 = bf16[1024,128]{1,0:T(8,128)(2,1)} custom-call(bf16[64,2,64,128]{3,2,1,0:T(8,128)(2,1)} %field_hbm.3, bf16[256,1024]{1,0:T(8,128)(2,1)} %constant.14.clone.depth_hbm, bf16[128,256]{1,0:T(8,128)(2,1)} %constant.15.clone.across_hbm), custom_call_target="tpu_custom_call" | custom-call | flops 536870912 | bytes 2097152 | tf_op jit(solution)/shard_map/field_analysis/pallas_call | solution.py:779
  4.9 7.4 %all-to-all-start = ((bf16[16,64,128]{2,1,0:T(8,128)(2,1)}), bf16[16,64,128]{2,1,0:T(8,128)(2,1)S(1)}, u32[]{:S(2)}, u32[]{:S(2)}) async-start(bf16[16,64,128]{2,1,0:T(8,128)(2,1)} %bitcast.17), calls=%async_computation | async-start | bytes 524288 | tf_op jit(solution)/shard_map/all_to_all | solution.py:757
  12.3 0.0 copy-start.1
  12.3 1.6 %copy-done.1 = bf16[64,2,64,128]{3,2,1,0:T(8,128)(2,1)S(1)} copy-done((bf16[64,2,64,128]{3,2,1,0:T(8,128)(2,1)S(1)}, bf16[64,2,64,128]{3,2,1,0:T(8,128)(2,1)}, u32[]{:S(2)}) %copy-start.1) | copy-done | bytes 2097176
  13.9 4.2 %channel_map.1.point_hbm = bf16[64,2,64,128]{3,2,1,0:T(8,128)(2,1)S(1)} custom-call(bf16[64,64]{1,0:T(8,128)(2,1)S(1)} %copy-done.15, bf16[64,2,64,128]{3,2,1,0:T(8,128)(2,1)S(1)} %copy-done.1), custom_call_target="tpu_custom_call" | custom-call | flops 2147483648 | bytes 4194304 | tf_op jit(solution)/shard_map/channel_map/pallas_call | solution.py:762
  18.1 4.2 %all-to-all-done = bf16[16,64,128]{2,1,0:T(8,128)(2,1)S(1)} async-done(((bf16[16,64,128]{2,1,0:T(8,128)(2,1)}), bf16[16,64,128]{2,1,0:T(8,128)(2,1)S(1)}, u32[]{:S(2)}, u32[]{:S(2)}) %all-to-all-start) | async-done | bytes 262176 | tf_op jit(solution)/shard_map/all_to_all | solution.py:757
  22.4 0.0 copy-start
  22.4 0.0 copy-start.2
  22.4 0.0 copy-start.5
  22.4 0.0 copy-start.6
  22.4 0.0 copy-start.12
  22.4 7.7 %mode_product.1 = (bf16[16,64,128]{2,1,0:T(8,128)(2,1)S(1)}, bf16[1024,128]{1,0:T(8,128)(2,1)S(1)}) custom-call(bf16[1024,128]{1,0:T(8,128)(2,1)S(1)} %bitcast.10, bf16[65536,128]{1,0:T(8,128)(2,1)} %bitcast.15, bf16[128,64]{1,0:T(8,128)(2,1)S(1)} %copy-done.10, bf16[64,64]{1,0:T(8,128)(2,1)S(1)} %copy-done.11, bf16[64,64]{1,0:T(8,128)(2,1)S(1)} %copy-done.8), custom_call_target="tpu_custom_call" | custom-call | flops 268435456 | bytes 17825792 | tf_op jit(solution)/shard_map/mode_product/pallas_call | solution.py:802
  30.2 0.7 copy-done.3
  30.9 12.8 %all_to_all.20 = bf16[16,64,128]{2,1,0:T(8,128)(2,1)S(1)} all-to-all(bf16[16,64,128]{2,1,0:T(8,128)(2,1)S(1)} %bitcast.14), channel_id=1, replica_groups=mesh['grp'=2,'gx'=16] {'gx'}, dimensions={0} | all-to-all | bytes 524288 | tf_op jit(solution)/shard_map/all_to_all | solution.py:757
  43.7 0.0 copy-done
  43.7 0.0 copy-done.5
  43.7 9.1 %gelu_and_gradient.1 = (bf16[64,2,64,128]{3,2,1,0:T(8,128)(2,1)}, bf16[64,2,64,128]{3,2,1,0:T(8,128)(2,1)S(1)}, bf16[1024,128]{1,0:T(8,128)(2,1)}) custom-call(bf16[1024,128]{1,0:T(8,128)(2,1)S(1)} %bitcast.12, f32[64]{0:T(128)S(1)} %copy-done.12, bf16[64,2,64,128]{3,2,1,0:T(8,128)(2,1)S(1)} %channel_map.1.point_hbm, bf16[64,2,64,128]{3,2,1,0:T(8,128)(2,1)S(1)} %copy-done.2, ...), custom_call_target="tpu_custom_call" | custom-call | flops 1073741824 | bytes 8388608 | tf_op jit(solution)/shard_map/gelu_and_gradient/pallas_call | solution.py:820
  52.9 0.0 copy-start.13
  52.9 1.3 %copy-done.13 = bf16[64,2,64,128]{3,2,1,0:T(8,128)(2,1)} copy-done((bf16[64,2,64,128]{3,2,1,0:T(8,128)(2,1)}, bf16[64,2,64,128]{3,2,1,0:T(8,128)(2,1)S(1)}, u32[]{:S(2)}) %copy-start.13) | copy-done | bytes 2097176
  54.2 3.7 %all-to-all-start.2 = ((bf16[16,64,128]{2,1,0:T(8,128)(2,1)}), bf16[16,64,128]{2,1,0:T(8,128)(2,1)S(1)}, u32[]{:S(2)}, u32[]{:S(2)}) async-start(bf16[16,64,128]{2,1,0:T(8,128)(2,1)} %bitcast.5), calls=%async_computation.2 | async-start | bytes 524288 | tf_op jit(solution)/shard_map/all_to_all | solution.py:757
  57.9 0.0 copy-start.14
  57.9 1.6 %copy-done.14 = bf16[64,2,64,128]{3,2,1,0:T(8,128)(2,1)S(1)} copy-done((bf16[64,2,64,128]{3,2,1,0:T(8,128)(2,1)S(1)}, bf16[64,2,64,128]{3,2,1,0:T(8,128)(2,1)}, u32[]{:S(2)}) %copy-start.14) | copy-done | bytes 2097176
  59.5 4.2 %channel_map_back.1.point_hbm = bf16[64,2,64,128]{3,2,1,0:T(8,128)(2,1)S(1)} custom-call(bf16[64,64]{1,0:T(8,128)(2,1)S(1)} %copy-done.15, bf16[64,2,64,128]{3,2,1,0:T(8,128)(2,1)S(1)} %copy-done.14), custom_call_target="tpu_custom_call" | custom-call | flops 2147483648 | bytes 4194304 | tf_op jit(solution)/shard_map/channel_map_back/pallas_call | solution.py:762
  63.7 4.0 %all-to-all-done.2 = bf16[16,64,128]{2,1,0:T(8,128)(2,1)S(1)} async-done(((bf16[16,64,128]{2,1,0:T(8,128)(2,1)}), bf16[16,64,128]{2,1,0:T(8,128)(2,1)S(1)}, u32[]{:S(2)}, u32[]{:S(2)}) %all-to-all-start.2) | async-done | bytes 262176 | tf_op jit(solution)/shard_map/all_to_all | solution.py:757
  67.7 7.6 %mode_gradient.1 = (bf16[32,64,128]{2,1,0:T(8,128)(2,1)S(1)}, bf16[1024,128]{1,0:T(8,128)(2,1)S(1)}) custom-call(bf16[1024,128]{1,0:T(8,128)(2,1)S(1)} %bitcast.9, bf16[65536,128]{1,0:T(8,128)(2,1)} %bitcast.16, bf16[128,64]{1,0:T(8,128)(2,1)S(1)} %copy-done.9, bf16[64,64]{1,0:T(8,128)(2,1)S(1)} %copy-done.8), custom_call_target="tpu_custom_call" | custom-call | flops 268435456 | bytes 17825792 | tf_op jit(solution)/shard_map/mode_gradient/pallas_call | solution.py:857
  75.4 0.0 copy-start.7
  75.4 0.7 copy-done.7
  76.1 3.5 %all-to-all-start.3 = ((bf16[16,64,128]{2,1,0:T(8,128)(2,1)}), bf16[16,64,128]{2,1,0:T(8,128)(2,1)S(1)}, u32[]{:S(2)}, u32[]{:S(2)}) async-start(bf16[16,64,128]{2,1,0:T(8,128)(2,1)} %bitcast.13), calls=%async_computation.3 | async-start | bytes 524288 | tf_op jit(solution)/shard_map/all_to_all | solution.py:757
  79.6 0.9 copy-done.4
  80.6 10.2 %weight_gradient.1 = bf16[1024,64,128]{2,1,0:T(8,128)(2,1)} custom-call(bf16[16,64,128]{2,1,0:T(8,128)(2,1)S(1)} %copy-done.4, bf16[32,64,128]{2,1,0:T(8,128)(2,1)S(1)} %get-tuple-element.24.pair_ref), custom_call_target="tpu_custom_call" | custom-call | flops 1073741824 | bytes 17825792 | tf_op jit(solution)/shard_map/weight_gradient/pallas_call | solution.py:869
  90.8 0.0 all-to-all-done.3
  90.8 3.6 %field_gradient.1 = bf16[64,2,64,128]{3,2,1,0:T(8,128)(2,1)} custom-call(bf16[1024,128]{1,0:T(8,128)(2,1)S(1)} %bitcast.11, bf16[64,2,64,128]{3,2,1,0:T(8,128)(2,1)S(1)} %channel_map_back.1.point_hbm, bf16[256,1024]{1,0:T(8,128)(2,1)S(1)} %copy-done, bf16[256,128]{1,0:T(8,128)(2,1)S(1)} %copy-done.5), custom_call_target="tpu_custom_call" | custom-call | flops 536870912 | bytes 4194304 | tf_op jit(solution)/shard_map/field_gradient/pallas_call | solution.py:884
  (15 shorter events, 0.0 us)
Async XLA Ops:
  0.6 11.7 %copy-start.15 = (bf16[64,64]{1,0:T(8,128)(2,1)S(1)}, bf16[64,64]{1,0:T(8,128)(2,1)}, u32[]{:S(2)}) copy-start(bf16[64,64]{1,0:T(8,128)(2,1)} %weight_ref.3) | copy-start | bytes 24580
  4.9 17.4 %all-to-all-start = ((bf16[16,64,128]{2,1,0:T(8,128)(2,1)}), bf16[16,64,128]{2,1,0:T(8,128)(2,1)S(1)}, u32[]{:S(2)}, u32[]{:S(2)}) async-start(bf16[16,64,128]{2,1,0:T(8,128)(2,1)} %bitcast.17), calls=%async_computation | async-start | bytes 524288 | tf_op jit(solution)/shard_map/all_to_all | solution.py:757
  12.3 1.6 %copy-start.1 = (bf16[64,2,64,128]{3,2,1,0:T(8,128)(2,1)S(1)}, bf16[64,2,64,128]{3,2,1,0:T(8,128)(2,1)}, u32[]{:S(2)}) copy-start(bf16[64,2,64,128]{3,2,1,0:T(8,128)(2,1)} %field_hbm.3) | copy-start | bytes 6291460
  13.9 8.4 %copy-start.8 = (bf16[64,64]{1,0:T(8,128)(2,1)S(1)}, bf16[64,64]{1,0:T(8,128)(2,1)}, u32[]{:S(2)}) copy-start(bf16[64,64]{1,0:T(8,128)(2,1)} %constant.20.clone.back_ref) | copy-start | bytes 24580
  13.9 8.4 %copy-start.10 = (bf16[128,64]{1,0:T(8,128)(2,1)S(1)}, bf16[128,64]{1,0:T(8,128)(2,1)}, u32[]{:S(2)}) copy-start(bf16[128,64]{1,0:T(8,128)(2,1)} %constant.18.clone.both_ref) | copy-start | bytes 49156
  13.9 8.4 %copy-start.11 = (bf16[64,64]{1,0:T(8,128)(2,1)S(1)}, bf16[64,64]{1,0:T(8,128)(2,1)}, u32[]{:S(2)}) copy-start(bf16[64,64]{1,0:T(8,128)(2,1)} %constant.17.clone.plain_ref) | copy-start | bytes 24580
  22.4 21.3 %copy-start = (bf16[256,1024]{1,0:T(8,128)(2,1)S(1)}, bf16[256,1024]{1,0:T(8,128)(2,1)}, u32[]{:S(2)}) copy-start(bf16[256,1024]{1,0:T(8,128)(2,1)} %constant.14.clone.depth_hbm) | copy-start | bytes 1572868
  22.4 21.3 %copy-start.2 = (bf16[64,2,64,128]{3,2,1,0:T(8,128)(2,1)S(1)}, bf16[64,2,64,128]{3,2,1,0:T(8,128)(2,1)}, u32[]{:S(2)}) copy-start(bf16[64,2,64,128]{3,2,1,0:T(8,128)(2,1)} %cot_hbm.1) | copy-start | bytes 6291460
  22.4 21.3 %copy-start.5 = (bf16[256,128]{1,0:T(8,128)(2,1)S(1)}, bf16[256,128]{1,0:T(8,128)(2,1)}, u32[]{:S(2)}) copy-start(bf16[256,128]{1,0:T(8,128)(2,1)} %constant.16.clone.back_hbm) | copy-start | bytes 196612
  22.4 21.3 %copy-start.6 = (bf16[128,256]{1,0:T(8,128)(2,1)S(1)}, bf16[128,256]{1,0:T(8,128)(2,1)}, u32[]{:S(2)}) copy-start(bf16[128,256]{1,0:T(8,128)(2,1)} %constant.15.clone.across_hbm) | copy-start | bytes 196612
  22.4 21.3 %copy-start.12 = (f32[64]{0:T(128)S(1)}, f32[64]{0:T(128)}, u32[]{:S(2)}) copy-start(f32[64]{0:T(128)} %bias_ref.1) | copy-start | bytes 772
  30.2 0.7 copy-start.3
  52.9 1.3 %copy-start.13 = (bf16[64,2,64,128]{3,2,1,0:T(8,128)(2,1)}, bf16[64,2,64,128]{3,2,1,0:T(8,128)(2,1)S(1)}, u32[]{:S(2)}) copy-start(bf16[64,2,64,128]{3,2,1,0:T(8,128)(2,1)S(1)} %get-tuple-element.19.field_hbm) | copy-start | bytes 6291460
  54.2 13.5 %all-to-all-start.2 = ((bf16[16,64,128]{2,1,0:T(8,128)(2,1)}), bf16[16,64,128]{2,1,0:T(8,128)(2,1)S(1)}, u32[]{:S(2)}, u32[]{:S(2)}) async-start(bf16[16,64,128]{2,1,0:T(8,128)(2,1)} %bitcast.5), calls=%async_computation.2 | async-start | bytes 524288 | tf_op jit(solution)/shard_map/all_to_all | solution.py:757
  57.9 1.6 %copy-start.14 = (bf16[64,2,64,128]{3,2,1,0:T(8,128)(2,1)S(1)}, bf16[64,2,64,128]{3,2,1,0:T(8,128)(2,1)}, u32[]{:S(2)}) copy-start(bf16[64,2,64,128]{3,2,1,0:T(8,128)(2,1)} %copy-done.13) | copy-start | bytes 6291460
  59.5 8.2 %copy-start.9 = (bf16[128,64]{1,0:T(8,128)(2,1)S(1)}, bf16[128,64]{1,0:T(8,128)(2,1)}, u32[]{:S(2)}) copy-start(bf16[128,64]{1,0:T(8,128)(2,1)} %constant.19.clone.straight_ref) | copy-start | bytes 49156
  75.4 0.7 copy-start.7
  76.1 14.7 %all-to-all-start.3 = ((bf16[16,64,128]{2,1,0:T(8,128)(2,1)}), bf16[16,64,128]{2,1,0:T(8,128)(2,1)S(1)}, u32[]{:S(2)}, u32[]{:S(2)}) async-start(bf16[16,64,128]{2,1,0:T(8,128)(2,1)} %bitcast.13), calls=%async_computation.3 | async-start | bytes 524288 | tf_op jit(solution)/shard_map/all_to_all | solution.py:757
  79.6 1.0 %copy-start.4 = (bf16[16,64,128]{2,1,0:T(8,128)(2,1)S(1)}, bf16[16,64,128]{2,1,0:T(8,128)(2,1)}, u32[]{:S(2)}) copy-start(bf16[16,64,128]{2,1,0:T(8,128)(2,1)} %copy-done.3) | copy-start | bytes 786436
where the time goes:
time: 95.2 us; the launch traced here: 94.6 us
  Pallas kernels  51 us (54%)
  starting transfers between devices  14.6 us (15%)
  blocking collectives  12.8 us (13%)
  waiting for transfers between devices  8.26 us (9%)
  local copies, waits for them, and re-layouts  6.89 us (7%)
  between operations  1.01 us (1%)
    all_to_all x3, starting transfers between devices, exchange(): lax.all_to_all(block.reshape(devices, 64, 128), 'gx', 0, 0, tiled=True)  14.6 us
    all_to_all x1, blocking collectives, exchange(): lax.all_to_all(block.reshape(devices, 64, 128), 'gx', 0, 0, tiled=True)  12.8 us
    pallas_call x1, Pallas kernels, fast_body(): pl.pallas_call(functools.partial(weight_grad_kernel, weight_scale), out_s...  10.2 us
    pallas_call x1, Pallas kernels, fast_body(): pl.pallas_call(functools.partial(middle_kernel, inverse_scale), out_shape...  9.13 us
    pallas_call x2, Pallas kernels, point(): pl.pallas_call(functools.partial(point_kernel, transposed), out_shape=fie...  8.4 us
    all_to_all x3, waiting for transfers between devices, exchange(): lax.all_to_all(block.reshape(devices, 64, 128), 'gx', 0, 0, tiled=True)  8.26 us
    pallas_call x1, Pallas kernels, fast_body(): pl.pallas_call(functools.partial(mode_kernel, forward_scale), out_shape=[...  7.73 us
    pallas_call x1, Pallas kernels, fast_body(): pl.pallas_call(functools.partial(mode_grad_kernel, forward_scale), out_sh...  7.62 us
  transfers between devices with their start and end apart: 3, of which 2 were waited for; matrix products, arithmetic and copies ran while one was open for 0% of the time, Pallas kernels for 20%

commit v1 on v0

--- a/solution.py
+++ b/solution.py
@@ -198,7 +198,7 @@
 PLANES = 2
 GROUP = 8
 STEP = 16
-VMEM_MIB = 40
+VMEM_MIB = 28
 NT = (((1,), (1,)), ((), ()))
 F32 = jnp.float32
 BF16 = jnp.bfloat16
@@ -493,6 +493,27 @@
 
     for step in range(steps):
         part_copy(out_ref, out_hbm, out_sems, step, STEP).wait()
+
+
+def load_and_point_kernel(
+    weight_ref,
+    field_hbm,
+    modes_hbm,
+    out_hbm,
+    modes_ref,
+    field_ref,
+    out_ref,
+    wide_ref,
+    in_sems,
+    out_sems,
+    mode_sems,
+):
+    copies = start_weights(modes_hbm, modes_ref, mode_sems)
+    point_kernel(
+        False, weight_ref, field_hbm, out_hbm, field_ref, out_ref, wide_ref, in_sems, out_sems
+    )
+    for copy in copies:
+        copy.wait()
 
 
 def point_kernel(
@@ -573,19 +594,16 @@
 def mode_kernel(
     scale,
     block_ref,
-    weight_hbm,
+    weight_ref,
     both_ref,
     plain_ref,
     back_ref,
     coeff_ref,
     out_ref,
-    weight_ref,
     rows_ref,
     left_ref,
     mixed_ref,
-    sems,
 ):
-    copies = start_weights(weight_hbm, weight_ref, sems)
     count = rows_ref.shape[0] // 16
     rows_ref[...] = block_ref[...].astype(F32)
     low = lanes((128, 128)) < 64
@@ -610,9 +628,6 @@
                 twice = jnp.where(low if h == 0 else ~low, coeffs, swapped).astype(BF16)
                 left_ref[j, h] = jnp.concatenate([twice * first, twice * second], axis=1)
     for j in range(16):
-        if j % 4 == 0:
-            for copy in copies[j : j + 4]:
-                copy.wait()
         mixed = []
         for u in range(MX // 8):
             halves = [
@@ -633,17 +648,14 @@
 def mode_grad_kernel(
     scale,
     block_ref,
-    weight_hbm,
+    weight_ref,
     straight_ref,
     back_ref,
     pair_ref,
     out_ref,
-    weight_ref,
     rows_ref,
     mixed_ref,
-    sems,
 ):
-    copies = start_weights(weight_hbm, weight_ref, sems)
     count = rows_ref.shape[0] // 16
     rows_ref[...] = block_ref[...].astype(F32)
     low = lanes((64, 128)) < 64
@@ -664,9 +676,6 @@
             part = turned[:, h * 128 : (h + 1) * 128]
             pair_ref[2 * j + h] = jnp.where(low, part[:64], part[64:]).astype(BF16)
     for j in range(16):
-        if j % 4 == 0:
-            for copy in copies[j : j + 4]:
-                copy.wait()
         mixed = []
         for u in range(MX // 8):
             found = []
@@ -685,29 +694,35 @@
 
 
 def weight_grad_kernel(scale, coeff_ref, pair_ref, out_hbm, out_ref, mask_ref, sems):
-    lane = lanes((128, 64))
-    part = sublanes((128, 64)) // 64
-    for t in range(MX // 4):
-        mask_ref[t] = ((lane // 8 == t) & (lane % 4 // 2 == part)).astype(BF16)
-    eye = (sublanes((128, 128)) == lanes((128, 128))).astype(BF16)
-    even = (sublanes((64, 128)) % 2 == 0).astype(BF16)
-    odd = (sublanes((64, 128)) % 2 == 1).astype(BF16)
+    lane = lanes((128, 128))
+    part = sublanes((128, 128)) // 64
+    for h in range(2):
+        for t in range(MX // 4):
+            mask_ref[h, t] = (
+                (lane // 64 == h) & (lane % 64 // 8 == t) & (lane % 4 // 2 == part)
+            ).astype(BF16)
+    low = (lanes((64, 128)) < 64).astype(BF16)
+    high = (lanes((64, 128)) >= 64).astype(BF16)
+    pick = (lanes((64, 128)) % 64 == sublanes((64, 128))).astype(BF16)
+    even = (sublanes((128, 128)) % 2 == 0).astype(BF16)
+    odd = (sublanes((128, 128)) % 2 == 1).astype(BF16)
 
     @pl.loop(0, 16)
     def _(j):
-        turned = (dot_nt(eye, coeff_ref[j]) * scale).astype(BF16)
+        coeffs = coeff_ref[j]
+        left = dot_nt(pick, jnp.concatenate([coeffs * low, coeffs * high], axis=0))
+        left = (left * scale).astype(BF16)
+        left = jnp.concatenate([left, left], axis=0)
+        pair = jnp.concatenate([pair_ref[j * 2], pair_ref[j * 2 + 1]], axis=0)
+        right = jnp.concatenate([pair * even, pair * odd], axis=1)
         for h in range(2):
-            left = turned[h * 64 : (h + 1) * 64]
-            left = jnp.concatenate([left, left], axis=0)
-            pair = pair_ref[j * 2 + h]
-            right = jnp.concatenate([pair * even, pair * odd], axis=1)
             for t in range(MX // 4):
-                four = dot_nn(left * mask_ref[t], right).astype(BF16)
+                four = dot_nn(left * mask_ref[h, t], right)
                 mode = (j * 2 + h) * MX + 4 * t
                 for k in range(4):
                     out_ref[mode + k] = four[
                         k // 2 * 64 : (k // 2 + 1) * 64, k % 2 * 128 : (k % 2 + 1) * 128
-                    ]
+                    ].astype(BF16)
         part_copy(out_ref, out_hbm, sems, j, 2 * MX).start()
 
     for j in range(16):
@@ -746,6 +761,9 @@
     def scratch(name):
         return pltpu.VMEM(table[name].shape, BF16)
 
+    def in_hbm(array):
+        return pltpu.with_memory_space_constraint(array, pltpu.HBM)
+
     steps = channels // STEP
     lines_scratch = pltpu.VMEM((MZ, channels, 2 * planes * lines), F32)
     rows_scratch = pltpu.VMEM((block_rows, 128), F32)
@@ -758,23 +776,13 @@
             block.reshape(devices, 64, 128), "gx", 0, 0, tiled=True
         ).reshape(block_rows, 128)
 
-    def point(field, transposed):
-        return pl.pallas_call(
-            functools.partial(point_kernel, transposed),
-            out_shape=field_shape,
-            in_specs=[vmem, hbm],
-            out_specs=hbm,
-            scratch_shapes=[
-                field_scratch,
-                field_scratch,
-                pltpu.VMEM((channels * 16, channels * 16), BF16),
-                sems(planes),
-                sems(planes),
-            ],
-            compiler_params=params(VMEM_MIB),
-            cost_estimate=cost(2 * 1024**3, 2 * field_bytes),
-            name="channel_map_back" if transposed else "channel_map",
-        )(channel_weight, field)
+    point_scratch = [
+        field_scratch,
+        field_scratch,
+        pltpu.VMEM((channels * 16, channels * 16), BF16),
+        sems(planes),
+        sems(planes),
+    ]
 
     block = pl.pallas_call(
         analysis_kernel,
@@ -790,28 +798,40 @@
             sems(steps),
             sems(2),
         ],
-        compiler_params=params(62),
+        compiler_params=params(28),
         cost_estimate=cost(2 * 256 * 1024 * 1024, field_bytes),
         name="field_analysis",
-    )(features, table["depth"], table["across_y"])
-    block, pointwise = lax.optimization_barrier((exchange(block), point(features, False)))
-
-    weight_scratch = pltpu.VMEM(weight_rows.shape, BF16)
+    )(in_hbm(features), table["depth"], table["across_y"])
+    pointwise, weight_rows = pl.pallas_call(
+        load_and_point_kernel,
+        out_shape=[
+            pltpu.HBM(features.shape, BF16),
+            pltpu.VMEM(weight_rows.shape, BF16),
+        ],
+        in_specs=[vmem, hbm, hbm],
+        out_specs=[hbm, vmem],
+        scratch_shapes=point_scratch + [sems(16)],
+        compiler_params=params(28),
+        cost_estimate=cost(2 * 1024**3, 2 * field_bytes + 2**24),
+        name="channel_map",
+    )(channel_weight, in_hbm(features), in_hbm(weight_rows))
+    block, pointwise, weight_rows = lax.optimization_barrier(
+        (exchange(block), pointwise, weight_rows)
+    )
+    weight_rows = pltpu.with_memory_space_constraint(weight_rows, pltpu.VMEM)
+
     mixed_scratch = pltpu.VMEM((16, 64, 128), BF16)
-    weight_sems = sems(16)
     coeffs, block = pl.pallas_call(
         functools.partial(mode_kernel, forward_scale),
         out_shape=[jax.ShapeDtypeStruct((16, 64, 128), BF16), block_shape],
-        in_specs=[vmem, hbm, vmem, vmem, vmem],
+        in_specs=[vmem, vmem, vmem, vmem, vmem],
         out_specs=[vmem, vmem],
         scratch_shapes=[
-            weight_scratch,
             rows_scratch,
             pltpu.VMEM((16, 2, 128, 256), BF16),
             mixed_scratch,
-            weight_sems,
         ],
-        compiler_params=params(VMEM_MIB),
+        compiler_params=params(24),
         cost_estimate=cost(256 * 2 * 16 * 256 * 128, 17 * 2**20),
         name="mode_product",
     )(block, weight_rows, table["both_x"], table["plain_x"], table["back_x"])
@@ -819,7 +839,7 @@
 
     activated, upstream, block = pl.pallas_call(
         functools.partial(middle_kernel, inverse_scale),
-        out_shape=[field_shape, field_shape, block_shape],
+        out_shape=[field_shape, pltpu.HBM(features.shape, BF16), block_shape],
         in_specs=[vmem, smem, hbm, hbm, hbm, hbm, hbm],
         out_specs=[hbm, hbm, vmem],
         scratch_shapes=[
@@ -845,22 +865,31 @@
     )(
         block,
         channel_bias,
-        pointwise,
-        cotangent,
+        in_hbm(pointwise),
+        in_hbm(cotangent),
         table["depth"],
         table["across_y"],
         table["back_y"],
     )
-    block = exchange(block)
-    block, channel_back = lax.optimization_barrier((block, point(upstream, True)))
+    channel_back = pl.pallas_call(
+        functools.partial(point_kernel, True),
+        out_shape=pltpu.HBM(features.shape, BF16),
+        in_specs=[vmem, hbm],
+        out_specs=hbm,
+        scratch_shapes=point_scratch,
+        compiler_params=params(28),
+        cost_estimate=cost(2 * 1024**3, 2 * field_bytes),
+        name="channel_map_back",
+    )(channel_weight, in_hbm(upstream))
+    block, channel_back = lax.optimization_barrier((exchange(block), channel_back))
 
     pairs, block = pl.pallas_call(
         functools.partial(mode_grad_kernel, forward_scale),
         out_shape=[jax.ShapeDtypeStruct((32, 64, 128), BF16), block_shape],
-        in_specs=[vmem, hbm, vmem, vmem],
+        in_specs=[vmem, vmem, vmem, vmem],
         out_specs=[vmem, vmem],
-        scratch_shapes=[weight_scratch, rows_scratch, mixed_scratch, weight_sems],
-        compiler_params=params(VMEM_MIB),
+        scratch_shapes=[rows_scratch, mixed_scratch],
+        compiler_params=params(24),
         cost_estimate=cost(256 * 2 * 16 * 256 * 128, 17 * 2**20),
         name="mode_gradient",
     )(block, weight_rows, table["straight_x"], table["back_x"])
@@ -873,7 +902,7 @@
         out_specs=hbm,
         scratch_shapes=[
             pltpu.VMEM(spectral_weight.shape, BF16),
-            pltpu.VMEM((MX // 4, 128, 64), BF16),
+            pltpu.VMEM((2, MX // 4, 128, 128), BF16),
             sems(16),
         ],
         compiler_params=params(VMEM_MIB),
@@ -900,7 +929,7 @@
         compiler_params=params(VMEM_MIB),
         cost_estimate=cost(2**29, 2 * field_bytes),
         name="field_gradient",
-    )(block, channel_back, table["depth"], table["back_y"])
+    )(block, in_hbm(channel_back), table["depth"], table["back_y"])
     return (activated, feature_grad, spectral_grad)
 
 

time: 95.2 us -> 108 us (1.13)
  local copies, waits for them, and re-layouts: 6.89 us -> 19.6 us
  waiting for transfers between devices: 8.26 us -> 5.02 us
  blocking collectives: 12.8 us -> 15.9 us
    unnamed x32 -> x28, local copies, waits for them, and re-layouts: 6.89 us -> 19.6 us
    pallas_call x2, Pallas kernels: 8.4 us -> 14.3 us  [the longest x1 9.49 us: fast_body(): pl.pallas_call(load_and_point_kernel, out_shape=[pltpu.HBM(features.shape...]
    pallas_call x1, Pallas kernels: 7.73 us -> 3.49 us  [fast_body(): pl.pallas_call(functools.partial(mode_kernel, forward_scale), out_shape=[...]
    all_to_all x3, waiting for transfers between devices: 8.26 us -> 5.02 us  [exchange(): lax.all_to_all(block.reshape(devices, 64, 128), 'gx', 0, 0, tiled=True)]
    all_to_all x1, blocking collectives: 12.8 us -> 15.9 us  [exchange(): lax.all_to_all(block.reshape(devices, 64, 128), 'gx', 0, 0, tiled=True)]
    pallas_call x1, Pallas kernels: 7.62 us -> 5.83 us  [fast_body(): pl.pallas_call(functools.partial(mode_grad_kernel, forward_scale), out_sh...]
  transfers between devices with their start and end apart: 3 -> 3, of which waited for: 2 -> 1; matrix products, arithmetic and copies ran while one was open for 0% -> 0% of each run, Pallas kernels for 20% -> 23%
where the time goes in v1:
time: 108 us
  Pallas kernels  51.7 us (48%)
  local copies, waits for them, and re-layouts  19.6 us (18%)
  blocking collectives  15.9 us (15%)
  starting transfers between devices  14.6 us (14%)
  waiting for transfers between devices  5.02 us (5%)
    unnamed x28, local copies, waits for them, and re-layouts  19.6 us
    all_to_all x1, blocking collectives, exchange(): lax.all_to_all(block.reshape(devices, 64, 128), 'gx', 0, 0, tiled=True)  15.9 us
    all_to_all x3, starting transfers between devices, exchange(): lax.all_to_all(block.reshape(devices, 64, 128), 'gx', 0, 0, tiled=True)  14.6 us
    pallas_call x1, Pallas kernels, fast_body(): pl.pallas_call(functools.partial(weight_grad_kernel, weight_scale), out_s...  10.5 us
    pallas_call x1, Pallas kernels, fast_body(): pl.pallas_call(functools.partial(middle_kernel, inverse_scale), out_shape...  9.54 us
    pallas_call x1, Pallas kernels, fast_body(): pl.pallas_call(load_and_point_kernel, out_shape=[pltpu.HBM(features.shape...  9.49 us
    pallas_call x1, Pallas kernels, fast_body(): pl.pallas_call(functools.partial(mode_grad_kernel, forward_scale), out_sh...  5.83 us
    all_to_all x3, waiting for transfers between devices, exchange(): lax.all_to_all(block.reshape(devices, 64, 128), 'gx', 0, 0, tiled=True)  5.02 us
  transfers between devices with their start and end apart: 3, of which 1 were waited for; matrix products, arithmetic and copies ran while one was open for 0% of the time, Pallas kernels for 23%

profile of v1, /device:TPU:0, one launch (start us, length us, event | category | flops | bytes accessed | tf_op | source)
XLA Modules:
  0.0 107.8 jit_solution(11750777238985494197)
XLA Ops:
  0.6 0.0 copy-start.3
  0.6 1.0 copy-done.3
  1.7 0.8 copy-done.6
  2.5 4.1 %field_analysis.1 = bf16[1024,128]{1,0:T(8,128)(2,1)} custom-call(bf16[64,2,64,128]{3,2,1,0:T(8,128)(2,1)} %field_hbm.3, bf16[256,1024]{1,0:T(8,128)(2,1)S(1)} %copy-done.3, bf16[128,256]{1,0:T(8,128)(2,1)S(1)} %copy-done.6), custom_call_target="tpu_custom_call" | custom-call | flops 536870912 | bytes 2097152 | tf_op jit(solution)/shard_map/field_analysis/pallas_call | solution.py:787
  6.6 7.4 %all-to-all-start = ((bf16[16,64,128]{2,1,0:T(8,128)(2,1)}), bf16[16,64,128]{2,1,0:T(8,128)(2,1)S(1)}, u32[]{:S(2)}, u32[]{:S(2)}) async-start(bf16[16,64,128]{2,1,0:T(8,128)(2,1)} %bitcast), calls=%async_computation | async-start | bytes 524288 | tf_op jit(solution)/shard_map/all_to_all | solution.py:775
  14.0 0.0 copy-done.11
  14.0 0.0 copy-start.8
  14.0 0.0 copy-start.10
  14.0 0.0 copy-start.12
  14.0 9.5 %channel_map.1 = (bf16[64,2,64,128]{3,2,1,0:T(8,128)(2,1)}, bf16[65536,128]{1,0:T(8,128)(2,1)S(1)}) custom-call(bf16[64,64]{1,0:T(8,128)(2,1)S(1)} %copy-done.11, bf16[64,2,64,128]{3,2,1,0:T(8,128)(2,1)} %field_hbm.3, bf16[65536,128]{1,0:T(8,128)(2,1)} %bitcast.14), custom_call_target="tpu_custom_call" | custom-call | flops 2147483648 | bytes 20971520 | tf_op jit(solution)/shard_map/channel_map/pallas_call | solution.py:805
  23.5 0.0 copy-start
  23.5 6.2 %copy-done = bf16[65536,128]{1,0:T(8,128)(2,1)} copy-done((bf16[65536,128]{1,0:T(8,128)(2,1)}, bf16[65536,128]{1,0:T(8,128)(2,1)S(1)}, u32[]{:S(2)}) %copy-start) | copy-done | bytes 16777240
  29.7 0.0 all-to-all-done
  29.7 0.0 copy-done.8
  29.7 0.0 copy-done.10
  29.7 0.0 copy-done.12
  29.7 0.0 copy-start.1
  29.7 5.8 %copy-done.1 = bf16[65536,128]{1,0:T(8,128)(2,1)S(1)} copy-done((bf16[65536,128]{1,0:T(8,128)(2,1)S(1)}, bf16[65536,128]{1,0:T(8,128)(2,1)}, u32[]{:S(2)}) %copy-start.1) | copy-done | bytes 16777240
  35.5 3.5 %mode_product.1 = (bf16[16,64,128]{2,1,0:T(8,128)(2,1)S(1)}, bf16[1024,128]{1,0:T(8,128)(2,1)S(1)}) custom-call(bf16[1024,128]{1,0:T(8,128)(2,1)S(1)} %bitcast.9, bf16[65536,128]{1,0:T(8,128)(2,1)S(1)} %copy-done.1, bf16[128,64]{1,0:T(8,128)(2,1)S(1)} %copy-done.10, bf16[64,64]{1,0:T(8,128)(2,1)S(1)} %copy-done.12, bf16[64,64]{1,0:T(8,128)(2,1)S(1)} %copy-done.8), custom_call_target="tpu_custom_call" | custom-call | flops 268435456 | bytes 17825792 | tf_op jit(solution)/shard_map/mode_product/pallas_call | solution.py:824
  39.0 15.9 %all_to_all.20 = bf16[16,64,128]{2,1,0:T(8,128)(2,1)S(1)} all-to-all(bf16[16,64,128]{2,1,0:T(8,128)(2,1)S(1)} %bitcast.13), channel_id=1, replica_groups=mesh['grp'=2,'gx'=16] {'gx'}, dimensions={0} | all-to-all | bytes 524288 | tf_op jit(solution)/shard_map/all_to_all | solution.py:775
  54.8 0.0 copy-done.5
  54.9 9.5 %gelu_and_gradient.1 = (bf16[64,2,64,128]{3,2,1,0:T(8,128)(2,1)}, bf16[64,2,64,128]{3,2,1,0:T(8,128)(2,1)}, bf16[1024,128]{1,0:T(8,128)(2,1)}) custom-call(bf16[1024,128]{1,0:T(8,128)(2,1)S(1)} %bitcast.12, f32[64]{0:T(128)S(1)} %copy-done.13, bf16[64,2,64,128]{3,2,1,0:T(8,128)(2,1)} %get-tuple-element.22.point_hbm, bf16[64,2,64,128]{3,2,1,0:T(8,128)(2,1)} %cot_hbm.1, ...), custom_call_target="tpu_custom_call" | custom-call | flops 1073741824 | bytes 8388608 | tf_op jit(solution)/shard_map/gelu_and_gradient/pallas_call | solution.py:840
  64.4 3.7 %all-to-all-start.2 = ((bf16[16,64,128]{2,1,0:T(8,128)(2,1)}), bf16[16,64,128]{2,1,0:T(8,128)(2,1)S(1)}, u32[]{:S(2)}, u32[]{:S(2)}) async-start(bf16[16,64,128]{2,1,0:T(8,128)(2,1)} %bitcast.5), calls=%async_computation.2 | async-start | bytes 524288 | tf_op jit(solution)/shard_map/all_to_all | solution.py:775
  68.1 0.0 copy-start.9
  68.2 4.8 %channel_map_back.1.point_hbm = bf16[64,2,64,128]{3,2,1,0:T(8,128)(2,1)} custom-call(bf16[64,64]{1,0:T(8,128)(2,1)S(1)} %copy-done.11, bf16[64,2,64,128]{3,2,1,0:T(8,128)(2,1)} %get-tuple-element.25.field_hbm), custom_call_target="tpu_custom_call" | custom-call | flops 2147483648 | bytes 4194304 | tf_op jit(solution)/shard_map/channel_map_back/pallas_call | solution.py:874
  73.0 5.0 %all-to-all-done.2 = bf16[16,64,128]{2,1,0:T(8,128)(2,1)S(1)} async-done(((bf16[16,64,128]{2,1,0:T(8,128)(2,1)}), bf16[16,64,128]{2,1,0:T(8,128)(2,1)S(1)}, u32[]{:S(2)}, u32[]{:S(2)}) %all-to-all-start.2) | async-done | bytes 262176 | tf_op jit(solution)/shard_map/all_to_all | solution.py:775
  78.0 5.8 %copy-done.2 = bf16[65536,128]{1,0:T(8,128)(2,1)S(1)} copy-done((bf16[65536,128]{1,0:T(8,128)(2,1)S(1)}, bf16[65536,128]{1,0:T(8,128)(2,1)}, u32[]{:S(2)}) %copy-start.2) | copy-done | bytes 16777240
  83.7 5.8 %mode_gradient.1 = (bf16[32,64,128]{2,1,0:T(8,128)(2,1)S(1)}, bf16[1024,128]{1,0:T(8,128)(2,1)}) custom-call(bf16[1024,128]{1,0:T(8,128)(2,1)S(1)} %bitcast.10, bf16[65536,128]{1,0:T(8,128)(2,1)S(1)} %copy-done.2, bf16[128,64]{1,0:T(8,128)(2,1)S(1)} %copy-done.9, bf16[64,64]{1,0:T(8,128)(2,1)S(1)} %copy-done.8), custom_call_target="tpu_custom_call" | custom-call | flops 268435456 | bytes 17825792 | tf_op jit(solution)/shard_map/mode_gradient/pallas_call | solution.py:886
  89.6 3.5 %all-to-all-start.3 = ((bf16[16,64,128]{2,1,0:T(8,128)(2,1)}), bf16[16,64,128]{2,1,0:T(8,128)(2,1)S(1)}, u32[]{:S(2)}, u32[]{:S(2)}) async-start(bf16[16,64,128]{2,1,0:T(8,128)(2,1)} %bitcast.7), calls=%async_computation.3 | async-start | bytes 524288 | tf_op jit(solution)/shard_map/all_to_all | solution.py:775
  93.1 10.5 %weight_gradient.1 = bf16[1024,64,128]{2,1,0:T(8,128)(2,1)} custom-call(bf16[16,64,128]{2,1,0:T(8,128)(2,1)S(1)} %get-tuple-element.29.coeff_ref, bf16[32,64,128]{2,1,0:T(8,128)(2,1)S(1)} %get-tuple-element.30.pair_ref), custom_call_target="tpu_custom_call" | custom-call | flops 1073741824 | bytes 17825792 | tf_op jit(solution)/shard_map/weight_gradient/pallas_call | solution.py:898
  103.7 0.0 all-to-all-done.3
  103.7 3.9 %field_gradient.1 = bf16[64,2,64,128]{3,2,1,0:T(8,128)(2,1)} custom-call(bf16[1024,128]{1,0:T(8,128)(2,1)S(1)} %bitcast.11, bf16[64,2,64,128]{3,2,1,0:T(8,128)(2,1)} %channel_map_back.1.point_hbm, bf16[256,1024]{1,0:T(8,128)(2,1)S(1)} %copy-done.4, bf16[256,128]{1,0:T(8,128)(2,1)S(1)} %copy-done.5), custom_call_target="tpu_custom_call" | custom-call | flops 536870912 | bytes 4194304 | tf_op jit(solution)/shard_map/field_gradient/pallas_call | solution.py:913
  (11 shorter events, 0.0 us)
Async XLA Ops:
  0.6 1.0 copy-start.3
  1.7 0.8 copy-start.6
  2.5 11.5 %copy-start.11 = (bf16[64,64]{1,0:T(8,128)(2,1)S(1)}, bf16[64,64]{1,0:T(8,128)(2,1)}, u32[]{:S(2)}) copy-start(bf16[64,64]{1,0:T(8,128)(2,1)} %weight_ref.3) | copy-start | bytes 24580
  6.6 23.1 %all-to-all-start = ((bf16[16,64,128]{2,1,0:T(8,128)(2,1)}), bf16[16,64,128]{2,1,0:T(8,128)(2,1)S(1)}, u32[]{:S(2)}, u32[]{:S(2)}) async-start(bf16[16,64,128]{2,1,0:T(8,128)(2,1)} %bitcast), calls=%async_computation | async-start | bytes 524288 | tf_op jit(solution)/shard_map/all_to_all | solution.py:775
  14.0 15.7 %copy-start.8 = (bf16[64,64]{1,0:T(8,128)(2,1)S(1)}, bf16[64,64]{1,0:T(8,128)(2,1)}, u32[]{:S(2)}) copy-start(bf16[64,64]{1,0:T(8,128)(2,1)} %constant.20.clone.back_ref) | copy-start | bytes 24580
  14.0 15.7 %copy-start.10 = (bf16[128,64]{1,0:T(8,128)(2,1)S(1)}, bf16[128,64]{1,0:T(8,128)(2,1)}, u32[]{:S(2)}) copy-start(bf16[128,64]{1,0:T(8,128)(2,1)} %constant.18.clone.both_ref) | copy-start | bytes 49156
  14.0 15.7 %copy-start.12 = (bf16[64,64]{1,0:T(8,128)(2,1)S(1)}, bf16[64,64]{1,0:T(8,128)(2,1)}, u32[]{:S(2)}) copy-start(bf16[64,64]{1,0:T(8,128)(2,1)} %constant.17.clone.plain_ref) | copy-start | bytes 24580
  23.5 6.2 %copy-start = (bf16[65536,128]{1,0:T(8,128)(2,1)}, bf16[65536,128]{1,0:T(8,128)(2,1)S(1)}, u32[]{:S(2)}) copy-start(bf16[65536,128]{1,0:T(8,128)(2,1)S(1)} %get-tuple-element.20.weight_ref) | copy-start | bytes 50331652
  29.7 5.8 %copy-start.1 = (bf16[65536,128]{1,0:T(8,128)(2,1)S(1)}, bf16[65536,128]{1,0:T(8,128)(2,1)}, u32[]{:S(2)}) copy-start(bf16[65536,128]{1,0:T(8,128)(2,1)} %copy-done) | copy-start | bytes 50331652
  35.5 19.4 %copy-start.4 = (bf16[256,1024]{1,0:T(8,128)(2,1)S(1)}, bf16[256,1024]{1,0:T(8,128)(2,1)}, u32[]{:S(2)}) copy-start(bf16[256,1024]{1,0:T(8,128)(2,1)} %constant.14.clone.depth_hbm) | copy-start | bytes 1572868
  35.5 19.4 %copy-start.5 = (bf16[256,128]{1,0:T(8,128)(2,1)S(1)}, bf16[256,128]{1,0:T(8,128)(2,1)}, u32[]{:S(2)}) copy-start(bf16[256,128]{1,0:T(8,128)(2,1)} %constant.16.clone.back_hbm) | copy-start | bytes 196612
  35.5 19.4 %copy-start.7 = (bf16[128,256]{1,0:T(8,128)(2,1)S(1)}, bf16[128,256]{1,0:T(8,128)(2,1)}, u32[]{:S(2)}) copy-start(bf16[128,256]{1,0:T(8,128)(2,1)} %constant.15.clone.across_hbm) | copy-start | bytes 196612
  35.5 19.4 %copy-start.13 = (f32[64]{0:T(128)S(1)}, f32[64]{0:T(128)}, u32[]{:S(2)}) copy-start(f32[64]{0:T(128)} %bias_ref.1) | copy-start | bytes 772
  64.4 13.6 %all-to-all-start.2 = ((bf16[16,64,128]{2,1,0:T(8,128)(2,1)}), bf16[16,64,128]{2,1,0:T(8,128)(2,1)S(1)}, u32[]{:S(2)}, u32[]{:S(2)}) async-start(bf16[16,64,128]{2,1,0:T(8,128)(2,1)} %bitcast.5), calls=%async_computation.2 | async-start | bytes 524288 | tf_op jit(solution)/shard_map/all_to_all | solution.py:775
  68.1 9.8 %copy-start.9 = (bf16[128,64]{1,0:T(8,128)(2,1)S(1)}, bf16[128,64]{1,0:T(8,128)(2,1)}, u32[]{:S(2)}) copy-start(bf16[128,64]{1,0:T(8,128)(2,1)} %constant.19.clone.straight_ref) | copy-start | bytes 49156
  78.0 5.8 %copy-start.2 = (bf16[65536,128]{1,0:T(8,128)(2,1)S(1)}, bf16[65536,128]{1,0:T(8,128)(2,1)}, u32[]{:S(2)}) copy-start(bf16[65536,128]{1,0:T(8,128)(2,1)} %copy-done) | copy-start | bytes 50331652
  89.6 14.1 %all-to-all-start.3 = ((bf16[16,64,128]{2,1,0:T(8,128)(2,1)}), bf16[16,64,128]{2,1,0:T(8,128)(2,1)S(1)}, u32[]{:S(2)}, u32[]{:S(2)}) async-start(bf16[16,64,128]{2,1,0:T(8,128)(2,1)} %bitcast.7), calls=%async_computation.3 | async-start | bytes 524288 | tf_op jit(solution)/shard_map/all_to_all | solution.py:775
